TPU v7x, 32 devices: a whole 2x2x4 slice. The times are simulated.
32 devices in a mesh: grp: 4 (over y, core), head: 8 (over z, x).
Axes of the slice: x: 2, y: 2, z: 4, core: 2. Of those that a mesh axis runs over, the one named last changes fastest.
Arguments:
- query_latent: bfloat16 [2048, 1536], P('grp'), may hold values from -6 to 6
- q_weight: bfloat16 [1536, 24576], P('grp', 'head'), may hold values from -0.15625 to 0.15625
- key_absorb: bfloat16 [128, 128, 512], P('head'), may hold values from -0.5 to 0.5
- value_up: bfloat16 [128, 512, 128], P('head'), may hold values from -0.25 to 0.25
- branch_latent: bfloat16 [4, 1536, 576], P('grp', 'head'), may hold values from -800 to 800, as said below
- lengths: int32 [4], P('grp'), may hold values from 512 to 1536, as said below
- row_depth: int32 [2048], P('grp'), may hold values from 1 to 1536
Outputs:
- attended: bfloat16 [2048, 16384], P('grp', 'head')
Inputs may be any that keep to these rules, and one draw needn't show every extreme that they name: `lengths`: every group has between 512 and 1536 live positions; some group has exactly 1536 and some other exactly 512. `branch_latent`: latent entries of order one.
All inputs are finite; a program needn't handle non-finite values.
Results may differ from a plain program's by a relative error of at most 0.012.
Values may be sent and summed in bfloat16 or wider, within the bound.
A program may use at most 128 MiB of HBM per device.

v0:
```python
import jax
import jax.numpy as jnp
from jax import lax
from jax.sharding import PartitionSpec as P

NOPE = 128
ROPE = 64
KVR = 512
VDIM = 128


def block_scores(queries, seen, latent, start, width, lower, upper, scale):
    block = lax.dynamic_slice_in_dim(latent, start, width, 0)
    score = (
        lax.dot_general(
            queries, block, (((1,), (1,)), ((), ())), preferred_element_type=jnp.float32
        )
        * scale
    )
    positions = start + jnp.arange(width, dtype=jnp.int32)
    inside = (positions >= lower) & (positions < upper)
    keep = inside[None, :] & (positions[None, :] < seen[:, None])
    return (score, keep, block)


def range_stats(queries, seen, latent, lower, upper, scale):
    width = latent.shape[0] // 4
    first = lower // width
    last = (upper + width - 1) // width

    def step(index, carry):
        peak, total = carry
        score, keep, block = block_scores(
            queries, seen, latent, index * width, width, lower, upper, scale
        )
        masked = jnp.where(keep, score, jnp.float32(-1e30))
        newer = jnp.maximum(peak, jnp.max(masked, axis=1))
        expo = jnp.where(keep, jnp.exp(score - newer[:, None]), jnp.float32(0.0))
        total = total * jnp.exp(peak - newer) + jnp.sum(expo, axis=1)
        return (newer, total)

    count = queries.shape[0]
    start_carry = (jnp.full((count,), -1e30, jnp.float32), jnp.zeros((count,), jnp.float32))
    return lax.fori_loop(first, jnp.maximum(last, first), step, start_carry)


def range_context(queries, seen, latent, lower, upper, peak, total, scale):
    width = latent.shape[0] // 4
    first = lower // width
    last = (upper + width - 1) // width

    def step(index, carry):
        score, keep, block = block_scores(
            queries, seen, latent, index * width, width, lower, upper, scale
        )
        weights = jnp.where(
            keep, jnp.exp(score - peak[:, None]) / total[:, None], jnp.float32(0.0)
        ).astype(jnp.bfloat16)
        return carry + jnp.dot(weights, block[:, :KVR], preferred_element_type=jnp.float32)

    start_carry = jnp.zeros((queries.shape[0], KVR), jnp.float32)
    return lax.fori_loop(first, jnp.maximum(last, first), step, start_carry)


def per_device(query_latent, q_weight, key_absorb, value_up, branch_latent, lengths, row_depth):
    scale = jnp.float32((NOPE + ROPE) ** (-0.5))
    row_count = query_latent.shape[0]
    head_count = key_absorb.shape[0]
    query = jnp.dot(
        query_latent,
        lax.all_gather(q_weight, "grp", axis=0, tiled=True),
        preferred_element_type=jnp.float32,
    ).astype(jnp.bfloat16)
    query = query.reshape(row_count, head_count, NOPE + ROPE)
    q_lat = jnp.einsum(
        "rhd,hdc->rhc", query[:, :, :NOPE], key_absorb, preferred_element_type=jnp.float32
    ).astype(jnp.bfloat16)
    q_abs = jnp.concatenate([q_lat, query[:, :, NOPE:]], axis=2)
    flat = q_abs.reshape(row_count * head_count, KVR + ROPE)
    latent = lax.all_gather(branch_latent, "head", axis=1, tiled=True)[0]
    limit = lengths[0]
    seen_own = jnp.repeat(row_depth, head_count)
    zero = jnp.int32(0)
    peak, total = range_stats(flat, seen_own, latent, zero, limit, scale)
    context = range_context(flat, seen_own, latent, zero, limit, peak, total, scale).astype(
        jnp.bfloat16
    )
    context = context.reshape(row_count, head_count, KVR)
    result = jnp.einsum("rhc,hcv->rhv", context, value_up, preferred_element_type=jnp.float32)
    return result.reshape(row_count, head_count * VDIM).astype(jnp.bfloat16)


def solution(mesh):
    placed = (
        P("grp", None),
        P("grp", "head"),
        P("head", None, None),
        P("head", None, None),
        P("grp", "head", None),
        P("grp"),
        P("grp"),
    )
    return jax.shard_map(
        per_device, mesh=mesh, in_specs=placed, out_specs=P("grp", "head"), check_vma=False
    )
```

profile of v0, /device:TPU:0, one launch (start us, length us, event | category | flops | bytes accessed | tf_op | source)
XLA Modules:
  0.0 341.3 jit_solution(4882267513563176123)
XLA Ops:
  8.7 67.2 %all-gather.5.cloned.1.call-done = bf16[1536,3072]{1,0:T(8,128)(2,1)} async-done(((bf16[384,3072]{1,0:T(8,128)(2,1)}), bf16[1536,3072]{1,0:T(8,128)(2,1)}) %all-gather.5.cloned.1.call-update) | async-done | bytes 9437200 | tf_op jit(solution)/shard_map/all_gather | solution.py:71
  75.9 9.3 %convolution_convert_fusion = bf16[512,3072]{1,0:T(8,128)(2,1)} fusion(bf16[512,1536]{1,0:T(8,128)(2,1)} %param.11, bf16[1536,3072]{1,0:T(8,128)(2,1)} %all-gather.5.cloned.1.call-done), kind=kOutput, calls=%fused_computation.29 | convolution fusion | flops 4833411072 | bytes 14155776 | tf_op jit(solution)/shard_map/dot_general | solution.py:69
  85.2 4.7 %copy.14 = bf16[512,3072]{0,1:T(8,128)(2,1)} copy(bf16[512,3072]{1,0:T(8,128)(2,1)} %convolution_convert_fusion) | data formatting | bytes 6291456 | tf_op jit(solution)/shard_map/convert_element_type | solution.py:73
  91.2 4.0 %convert_bitcast_fusion = bf16[512,16,512]{0,2,1:T(8,128)(2,1)S(1)} fusion(bf16[16,128,512]{2,1,0:T(8,128)(2,1)S(1)} %copy-done, bf16[512,16,192]{0,2,1:T(8,128)(2,1)} %bitcast.45), kind=kOutput, calls=%fused_computation.28 | convolution fusion | flops 1077936128 | bytes 12582912 | tf_op jit(solution)/shard_map/rhd,hdc->rhc/dot_general | solution.py:75
  95.2 4.0 %pad_maximum_fusion = bf16[512,16,576]{0,2,1:T(8,128)(2,1)} fusion(bf16[512,16,64]{0,2,1:T(8,128)(2,1)S(1)} %slice.13, bf16[512,16,512]{0,2,1:T(8,128)(2,1)S(1)} %convert_bitcast_fusion), kind=kLoop, calls=%fused_computation.25 | loop fusion | flops 18874368 | bytes 18874368 | tf_op jit(solution)/shard_map/concatenate | solution.py:78
  99.1 17.5 %copy.17 = bf16[512,16,576]{2,1,0:T(8,128)(2,1)} copy(bf16[512,16,576]{0,2,1:T(8,128)(2,1)} %pad_maximum_fusion) | data formatting | bytes 18874368 | tf_op jit(solution)/shard_map/concatenate | solution.py:78
  116.7 9.0 %all-gather.3.cloned.1.call-done = bf16[1,1536,576]{2,1,0:T(8,128)(2,1)} async-done(((bf16[1,192,576]{2,1,0:T(8,128)(2,1)}), bf16[1,1536,576]{2,1,0:T(8,128)(2,1)}) %all-gather.3.cloned.1.call-update) | async-done | bytes 1769488 | tf_op jit(solution)/shard_map/all_gather | solution.py:80
  125.6 90.5 %while.24 = (s32[]{:T(128)}, f32[8192]{0:T(1024)S(1)}, f32[8192]{0:T(1024)S(1)}, s32[]{:T(128)}, s32[]{:T(128)}, /*index=5*/bf16[1536,576]{1,0:T(8,128)(2,1)}, b...) while((s32[]{:T(128)}, f32[8192]{0:T(1024)S(1)}, ...), condition=%wide.region_3.4_spmd.clone, body=%wide.region_0.3_spmd.clone.sunk | while | flops 3655354368 | bytes 36740912 | solution.py:44
  126.8 14.6 %fusion.37 = (f32[8192]{0:T(1024)S(1)}, f32[384,8192]{1,0:T(8,128)}) fusion(s32[8192]{0:T(1024)S(1)} %lt.127, s32[384]{0:T(512)S(1)} %iota_add_fusion.4, pred[384]{0:T(512)(128)(4,1)S(1)} %compare_and_fusion.5, bf16[8192,576]{1,0:T(8,128)(2,1)} %get-tuple-element.318, bf16[1536,576]{1,0:T(8,128)(2,1)} %get-tuple-element.317, s32[]{:T(128)S(6)} %select_n.48), kind=kOutput, calls=%fused_computation.4.clone.1 | convolution fusion | flops 3639599104 | bytes 23627652 | tf_op jit(solution)/shard_map/while/body/dot_general | solution.py:15
  141.3 7.0 %fusion.38 = f32[8192]{0:T(1024)S(1)} fusion(f32[384,8192]{1,0:T(8,128)} %get-tuple-element.278, f32[8192]{0:T(1024)S(1)} %max.10, s32[8192]{0:T(1024)S(1)} %lt.127, s32[384]{0:T(512)S(1)} %iota_add_fusion.4, pred[384]{0:T(512)(128)(4,1)S(1)} %compare_and_fusion.5), kind=kLoop, calls=%fused_computation.7.clone.1 | loop fusion | flops 15720448 | bytes 12683136 | tf_op jit(solution)/shard_map/while/body/reduce_sum | solution.py:39
  149.4 14.6 %fusion.37 = (f32[8192]{0:T(1024)S(1)}, f32[384,8192]{1,0:T(8,128)}) fusion(s32[8192]{0:T(1024)S(1)} %lt.127, s32[384]{0:T(512)S(1)} %iota_add_fusion.4, pred[384]{0:T(512)(128)(4,1)S(1)} %compare_and_fusion.5, bf16[8192,576]{1,0:T(8,128)(2,1)} %get-tuple-element.318, bf16[1536,576]{1,0:T(8,128)(2,1)} %get-tuple-element.317, s32[]{:T(128)S(6)} %select_n.48), kind=kOutput, calls=%fused_computation.4.clone.1 | convolution fusion | flops 3639599104 | bytes 23627652 | tf_op jit(solution)/shard_map/while/body/dot_general | solution.py:15
  163.9 7.0 %fusion.38 = f32[8192]{0:T(1024)S(1)} fusion(f32[384,8192]{1,0:T(8,128)} %get-tuple-element.278, f32[8192]{0:T(1024)S(1)} %max.10, s32[8192]{0:T(1024)S(1)} %lt.127, s32[384]{0:T(512)S(1)} %iota_add_fusion.4, pred[384]{0:T(512)(128)(4,1)S(1)} %compare_and_fusion.5), kind=kLoop, calls=%fused_computation.7.clone.1 | loop fusion | flops 15720448 | bytes 12683136 | tf_op jit(solution)/shard_map/while/body/reduce_sum | solution.py:39
  171.9 14.6 %fusion.37 = (f32[8192]{0:T(1024)S(1)}, f32[384,8192]{1,0:T(8,128)}) fusion(s32[8192]{0:T(1024)S(1)} %lt.127, s32[384]{0:T(512)S(1)} %iota_add_fusion.4, pred[384]{0:T(512)(128)(4,1)S(1)} %compare_and_fusion.5, bf16[8192,576]{1,0:T(8,128)(2,1)} %get-tuple-element.318, bf16[1536,576]{1,0:T(8,128)(2,1)} %get-tuple-element.317, s32[]{:T(128)S(6)} %select_n.48), kind=kOutput, calls=%fused_computation.4.clone.1 | convolution fusion | flops 3639599104 | bytes 23627652 | tf_op jit(solution)/shard_map/while/body/dot_general | solution.py:15
  186.5 7.0 %fusion.38 = f32[8192]{0:T(1024)S(1)} fusion(f32[384,8192]{1,0:T(8,128)} %get-tuple-element.278, f32[8192]{0:T(1024)S(1)} %max.10, s32[8192]{0:T(1024)S(1)} %lt.127, s32[384]{0:T(512)S(1)} %iota_add_fusion.4, pred[384]{0:T(512)(128)(4,1)S(1)} %compare_and_fusion.5), kind=kLoop, calls=%fused_computation.7.clone.1 | loop fusion | flops 15720448 | bytes 12683136 | tf_op jit(solution)/shard_map/while/body/reduce_sum | solution.py:39
  194.5 14.6 %fusion.37 = (f32[8192]{0:T(1024)S(1)}, f32[384,8192]{1,0:T(8,128)}) fusion(s32[8192]{0:T(1024)S(1)} %lt.127, s32[384]{0:T(512)S(1)} %iota_add_fusion.4, pred[384]{0:T(512)(128)(4,1)S(1)} %compare_and_fusion.5, bf16[8192,576]{1,0:T(8,128)(2,1)} %get-tuple-element.318, bf16[1536,576]{1,0:T(8,128)(2,1)} %get-tuple-element.317, s32[]{:T(128)S(6)} %select_n.48), kind=kOutput, calls=%fused_computation.4.clone.1 | convolution fusion | flops 3639599104 | bytes 23627652 | tf_op jit(solution)/shard_map/while/body/dot_general | solution.py:15
  209.1 7.0 %fusion.38 = f32[8192]{0:T(1024)S(1)} fusion(f32[384,8192]{1,0:T(8,128)} %get-tuple-element.278, f32[8192]{0:T(1024)S(1)} %max.10, s32[8192]{0:T(1024)S(1)} %lt.127, s32[384]{0:T(512)S(1)} %iota_add_fusion.4, pred[384]{0:T(512)(128)(4,1)S(1)} %compare_and_fusion.5), kind=kLoop, calls=%fused_computation.7.clone.1 | loop fusion | flops 15720448 | bytes 12683136 | tf_op jit(solution)/shard_map/while/body/reduce_sum | solution.py:39
  216.1 7.9 %broadcast_in_dim.29 = f32[8192,512]{1,0:T(8,128)} broadcast(f32[]{:T(128)} %constant.60.clone.1), dimensions={} | broadcast | bytes 16777220 | tf_op jit(solution)/shard_map/broadcast_in_dim | solution.py:61
  224.0 83.2 %while.25 = (s32[]{:T(128)}, f32[8192,512]{1,0:T(8,128)}, s32[]{:T(128)}, s32[]{:T(128)}, bf16[1536,576]{1,0:T(8,128)(2,1)}, /*index=5*/bf16[8192,576]{1,0:T(8,1...) while((s32[]{:T(128)}, f32[8192,512]{1,0:T(8,128)}, ...), condition=%wide.region_5.6_spmd.clone, body=%wide.region_4.5_spmd.clone.sunk | while | flops 6871320576 | bytes 45128632 | solution.py:62
  224.9 19.8 %convolution_add_fusion.2 = f32[8192,512]{1,0:T(8,128)} fusion(f32[8192,512]{1,0:T(8,128)} %get-tuple-element.338, bf16[8192,576]{1,0:T(8,128)(2,1)} %get-tuple-element.355, f32[8192]{0:T(1024)S(1)} %get-tuple-element.357, f32[8192]{0:T(1024)S(1)} %get-tuple-element.356, s32[384]{0:T(512)S(1)} %iota_add_fusion.5, s32[8192]{0:T(1024)S(1)} %lt.134, ...), kind=kOutput, calls=%fused_computation.17.clone.1 | convolution fusion | flops 6871318528 | bytes 45026176 | tf_op jit(solution)/shard_map/while/body/dot_general | solution.py:59
  245.7 19.8 %convolution_add_fusion.2 = f32[8192,512]{1,0:T(8,128)} fusion(f32[8192,512]{1,0:T(8,128)} %get-tuple-element.338, bf16[8192,576]{1,0:T(8,128)(2,1)} %get-tuple-element.355, f32[8192]{0:T(1024)S(1)} %get-tuple-element.357, f32[8192]{0:T(1024)S(1)} %get-tuple-element.356, s32[384]{0:T(512)S(1)} %iota_add_fusion.5, s32[8192]{0:T(1024)S(1)} %lt.134, ...), kind=kOutput, calls=%fused_computation.17.clone.1 | convolution fusion | flops 6871318528 | bytes 45026176 | tf_op jit(solution)/shard_map/while/body/dot_general | solution.py:59
  266.5 19.9 %convolution_add_fusion.2 = f32[8192,512]{1,0:T(8,128)} fusion(f32[8192,512]{1,0:T(8,128)} %get-tuple-element.338, bf16[8192,576]{1,0:T(8,128)(2,1)} %get-tuple-element.355, f32[8192]{0:T(1024)S(1)} %get-tuple-element.357, f32[8192]{0:T(1024)S(1)} %get-tuple-element.356, s32[384]{0:T(512)S(1)} %iota_add_fusion.5, s32[8192]{0:T(1024)S(1)} %lt.134, ...), kind=kOutput, calls=%fused_computation.17.clone.1 | convolution fusion | flops 6871318528 | bytes 45026176 | tf_op jit(solution)/shard_map/while/body/dot_general | solution.py:59
  287.3 19.9 %convolution_add_fusion.2 = f32[8192,512]{1,0:T(8,128)} fusion(f32[8192,512]{1,0:T(8,128)} %get-tuple-element.338, bf16[8192,576]{1,0:T(8,128)(2,1)} %get-tuple-element.355, f32[8192]{0:T(1024)S(1)} %get-tuple-element.357, f32[8192]{0:T(1024)S(1)} %get-tuple-element.356, s32[384]{0:T(512)S(1)} %iota_add_fusion.5, s32[8192]{0:T(1024)S(1)} %lt.134, ...), kind=kOutput, calls=%fused_computation.17.clone.1 | convolution fusion | flops 6871318528 | bytes 45026176 | tf_op jit(solution)/shard_map/while/body/dot_general | solution.py:59
  307.2 9.2 %convert_element_type.27 = bf16[8192,512]{1,0:T(8,128)(2,1)} convert(f32[8192,512]{1,0:T(8,128)} %get-tuple-element.99) | non-fusion elementwise | flops 4194304 | bytes 25165824 | tf_op jit(solution)/shard_map/convert_element_type | solution.py:85
  316.3 14.2 %fusion.21 = bf16[16,512,128]{1,2,0:T(8,128)(2,1)} fusion(bf16[16,512,128]{2,1,0:T(8,128)(2,1)S(1)} %copy-done.3, bf16[512,16,512]{2,1,0:T(8,128)(2,1)} %bitcast.47), kind=kOutput, calls=%fused_computation.31 | convolution fusion | flops 1074790400 | bytes 12582912 | tf_op jit(solution)/shard_map/rhc,hcv->rhv/dot_general | solution.py:89
  (60 shorter events, 14.1 us)
Async XLA Ops:
  6.5 84.6 %copy-start = (bf16[16,128,512]{2,1,0:T(8,128)(2,1)S(1)}, bf16[16,128,512]{2,1,0:T(8,128)(2,1)}, u32[]{:S(2)}) copy-start(bf16[16,128,512]{2,1,0:T(8,128)(2,1)} %param.13) | copy-start | bytes 6291460
  6.5 69.4 %all-gather.5.cloned.1.call-start = ((), (), s32[]{:S(2)}) async-start(), calls=%async_computation.1 | async-start | bytes 11796480 | tf_op jit(solution)/shard_map/all_gather | solution.py:71
  7.3 118.4 %all-gather.3.cloned.1.call-start = ((), (), s32[]{:S(2)}) async-start(), calls=%async_computation | async-start | bytes 2211840 | tf_op jit(solution)/shard_map/all_gather | solution.py:80
  99.1 26.5 %copy-start.2 = (s32[512]{0:T(512)S(1)}, s32[512]{0:T(512)}, u32[]{:S(2)}) copy-start(s32[512]{0:T(512)} %param.17) | copy-start | bytes 6148
  307.2 9.2 %copy-start.3 = (bf16[16,512,128]{2,1,0:T(8,128)(2,1)S(1)}, bf16[16,512,128]{2,1,0:T(8,128)(2,1)}, u32[]{:S(2)}) copy-start(bf16[16,512,128]{2,1,0:T(8,128)(2,1)} %param.14) | copy-start | bytes 6291460
  316.3 18.1 %copy-start.1 = (bf16[16,128,512]{2,1,0:T(8,128)(2,1)S(1)}, bf16[16,128,512]{2,1,0:T(8,128)(2,1)}, u32[]{:S(2)}) copy-start(bf16[16,128,512]{2,1,0:T(8,128)(2,1)} %param.13) | copy-start | bytes 6291460
Sparse Core Ops, SparseCore 0:
  8.9 66.9 all-gather.4
  78.1 47.5 all-gather.2
where the time goes:
time: 342 us; the launch traced here: 341 us
  matrix products  165 us (48%)
  waiting for transfers between devices  77.6 us (23%)
  other arithmetic  46.5 us (14%)
  local copies, waits for them, and re-layouts  37.3 us (11%)
  between operations  14.1 us (4%)
    dot_general x4, matrix products, step(): jnp.dot(weights, block[:, :KVR], preferred_element_type=jnp.float32)  79.4 us
    all_gather x1, waiting for transfers between devices, per_device(): lax.all_gather(q_weight, 'grp', axis=0, tiled=True)  67.2 us
    dot_general x4, matrix products, block_scores(): lax.dot_general(queries, block, (((1,), (1,)), ((), ())), preferred_eleme...  58.2 us
    reduce_sum x4, other arithmetic, step(): total = total * jnp.exp(peak - newer) + jnp.sum(expo, axis=1)  28 us
    concatenate x1, local copies, waits for them, and re-layouts, per_device(): q_abs = jnp.concatenate([q_lat, query[:, :, NOPE:]], axis=2)  17.5 us
    dot_general x1, matrix products, per_device(): jnp.einsum('rhc,hcv->rhv', context, value_up, preferred_element_type=jnp....  14.2 us
    dot_general x1, matrix products, per_device(): jnp.dot(query_latent, lax.all_gather(q_weight, 'grp', axis=0, tiled=True)...  9.3 us
    convert_element_type x1, other arithmetic, per_device(): range_context(flat, seen_own, latent, zero, limit, peak, total, scale)  9.16 us
  transfers between devices with their start and end apart: 2, of which 2 were waited for; matrix products, arithmetic and copies ran while one was open for 12% of the time, Pallas kernels for 0%

commit v1 on v0

v1 whole, which is shorter than its diff:
```python
import functools
import math

import jax
import jax.numpy as jnp
from jax import lax
from jax.experimental import pallas as pl
from jax.experimental.pallas import tpu as pltpu
from jax.sharding import PartitionSpec as P

NOPE = 128
ROPE = 64
KVR = 512
VDIM = 128
HEAD = NOPE + ROPE
PAIR = 2 * HEAD
WIDE = 256
AHEAD = 3
MESH = pl.DeviceIdType.MESH
NT = (((1,), (1,)), ((), ()))
SCALE = (HEAD ** -0.5) * math.log2(math.e)


def kernel(Y, Z, X, ql_h, w_h, ka_h, vu_h, lat_h, dep, lens, out_h,
           wbuf, ql, ka, vu, lat, kt, vv, obuf, qb, seen,
           ysend, yrecv, csend, crecv, fsend, frecv,
           zsend, zrecv, xsend, xrecv, lsem, vsem, osem):
    rows, rank = ql.shape
    depth, cols = w_h.shape
    heads = vu_h.shape[0]
    share = lat_h.shape[0]
    length = lat.shape[0]
    pieces = cols // PAIR
    chunk = 128 * share // math.gcd(128, share)
    chunks = length // chunk
    whole_rows = chunk == X * share
    g, h = lax.axis_index("grp"), lax.axis_index("head")
    y, c = lax.div(g, 2), lax.rem(g, 2)
    z, x = lax.div(h, X), lax.rem(h, X)

    def y_at(d):
        return {"grp": lax.rem(y + d, Y) * 2 + c, "head": h}

    other = {"grp": y * 2 + 1 - c, "head": h}

    def z_at(d):
        return {"grp": g, "head": lax.rem(z + d, Z) * X + x}

    def x_at(d):
        return {"grp": g, "head": z * X + lax.rem(x + d, X)}

    def w_part(owner, j):
        return wbuf.at[pl.ds(pl.multiple_of(owner * depth, 16), depth),
                       pl.ds(pl.multiple_of(j * PAIR, 128), PAIR)]

    def w_own(j):
        return w_h.at[:, pl.ds(pl.multiple_of(j * PAIR, 128), PAIR)]

    def shard(index):
        return lat.at[pl.ds(pl.multiple_of(index * share, 16), share)]

    def remote(src, dst, send, recv, to):
        return pltpu.make_async_remote_copy(
            src_ref=src, dst_ref=dst, send_sem=send, recv_sem=recv,
            device_id=to, device_id_type=MESH)

    def y_copy(j, d):
        return remote(w_own(j), w_part(g, j), ysend.at[d - 1, j], yrecv.at[d - 1, j], y_at(d))

    def c_copy(j):
        return remote(w_own(j), w_part(g, j), csend.at[j], crecv.at[j], other)

    def f_copy(j, d):
        part = w_part(lax.rem(y + Y - d, Y) * 2 + c, j)
        return remote(part, part, fsend.at[d - 1, j], frecv.at[d - 1, j], other)

    def z_copy(d):
        return remote(lat_h, shard(h), zsend.at[d - 1], zrecv.at[d - 1], z_at(d))

    def x_copy(dz, dx):
        if dz == 0:
            src, dst = lat_h, shard(h)
        else:
            src = dst = shard(lax.rem(z + Z - dz, Z) * X + x)
        return remote(src, dst, xsend.at[dz, dx - 1], xrecv.at[dz, dx - 1], x_at(dx))

    peers = ([y_at(d) for d in range(1, Y)] + [other]
             + [z_at(d) for d in range(1, Z)] + [x_at(d) for d in range(1, X)])
    barrier = pltpu.get_barrier_semaphore()
    for peer in peers:
        pl.semaphore_signal(barrier, inc=1, device_id=peer, device_id_type=MESH)

    local = [
        pltpu.make_async_copy(lat_h, shard(h), lsem.at[0]),
        pltpu.make_async_copy(ka_h, ka, lsem.at[1]),
        pltpu.make_async_copy(ql_h, ql, lsem.at[2]),
        pltpu.make_async_copy(w_h, wbuf.at[pl.ds(pl.multiple_of(g * depth, 16), depth)], lsem.at[3]),
    ]
    for i in range(heads):
        local.append(pltpu.make_async_copy(vu_h.at[i], vu.at[:, pl.ds(i * VDIM, VDIM)], vsem.at[i]))
    for copy in local:
        copy.start()
    pl.semaphore_wait(barrier, len(peers))

    def start_piece(j):
        for d in range(1, Y):
            y_copy(j, d).start()
        c_copy(j).start()

    start_piece(0)
    for dx in range(1, X):
        x_copy(0, dx).start()
    for d in range(1, Z):
        z_copy(d).start()
    for j in range(1, min(AHEAD, pieces)):
        start_piece(j)

    row = lax.broadcasted_iota(jnp.int32, (rows, rows), 0)
    col = lax.broadcasted_iota(jnp.int32, (rows, rows), 1)
    kept = jnp.minimum(dep[...], lens[0]).astype(jnp.float32)
    seen[...] = jnp.sum(jnp.where(row == col, kept, 0.0), axis=1, keepdims=True).astype(jnp.int32)

    for copy in local:
        copy.wait()

    eye = (lax.broadcasted_iota(jnp.int32, (ROPE, ROPE), 0)
           == lax.broadcasted_iota(jnp.int32, (ROPE, ROPE), 1)).astype(jnp.bfloat16)
    at_once = 4

    def keys_values(index):
        at = pl.ds(pl.multiple_of(index * chunk, 128), chunk)
        rope = lax.dot_general(eye, lat[at, KVR:], NT, preferred_element_type=jnp.float32).astype(jnp.bfloat16)
        blank = jnp.zeros((ROPE, chunk), jnp.bfloat16)

        @pl.loop(0, heads // at_once)
        def _(i):
            latent = lat[at, :KVR]
            wide = at_once * NOPE
            keys = lax.dot_general(ka[pl.ds(pl.multiple_of(i * wide, 16), wide), :], latent, NT,
                                   preferred_element_type=jnp.float32).astype(jnp.bfloat16)
            for e in range(at_once):
                own = keys[e * NOPE:(e + 1) * NOPE]
                head = i * at_once + e
                if e % 2 == 0:
                    kt[head, 0:NOPE, at] = own
                    kt[head, NOPE:HEAD, at] = rope
                    kt[head, HEAD:WIDE, at] = blank
                else:
                    kt[head, 0:ROPE, at] = blank
                    kt[head, ROPE:HEAD, at] = own
                    kt[head, HEAD:WIDE, at] = rope
            over = pl.ds(pl.multiple_of(i * wide, 128), wide)
            vv[at, over] = jnp.dot(latent, vu[:, over], preferred_element_type=jnp.float32).astype(jnp.bfloat16)

    def take_x(dz):
        for dx in range(1, X):
            x_copy(dz, dx).wait_recv()

    def pass_on(dz):
        z_copy(dz).wait_recv()
        for dx in range(1, X):
            x_copy(dz, dx).start()

    waited = 0
    started = min(AHEAD, pieces)
    if not whole_rows:
        for dz in range(1, Z):
            pass_on(dz)
        for dz in range(Z):
            take_x(dz)
    for k in range(chunks):
        if whole_rows:
            if k + 1 < Z:
                pass_on(k + 1)
            take_x(k)
            keys_values(lax.rem(z + Z - k, Z))
        else:
            keys_values(k)
        if started < pieces:
            for d in range(1, Y):
                y_copy(waited, d).wait_send()
            waited += 1
            start_piece(started)
            started += 1
    while started < pieces:
        start_piece(started)
        started += 1

    half = rows // 2
    ones = jnp.ones((length, VDIM), jnp.bfloat16)

    @pl.loop(0, pieces)
    def _(j):
        for d in range(1, Y):
            y_copy(j, d).wait_recv()
            f_copy(j, d).start()
        c_copy(j).wait_recv()
        for d in range(1, Y):
            f_copy(j, d).wait_recv()
        weight = pl.ds(pl.multiple_of(j * PAIR, 128), PAIR)
        for r in range(2):
            part = slice(r * half, (r + 1) * half)
            q = jnp.dot(ql[part, :], wbuf[:, weight], preferred_element_type=jnp.float32)
            qb[part, :] = (q * jnp.float32(SCALE)).astype(jnp.bfloat16)
        for r in range(2):
            part = slice(r * half, (r + 1) * half)
            limit = seen[part, :]
            for e in range(2):
                head = j * 2 + e
                q = qb[part, 0:WIDE] if e == 0 else qb[part, NOPE:PAIR]
                s = jnp.dot(q, kt[head], preferred_element_type=jnp.float32)
                place = lax.broadcasted_iota(jnp.int32, s.shape, 1)
                s = jnp.where(place < limit, s, jnp.float32(-1e30))
                peak = jnp.max(s, axis=1, keepdims=True)
                p = jnp.exp2(s - peak).astype(jnp.bfloat16)
                over = pl.ds(pl.multiple_of(head * VDIM, 128), VDIM)
                both = jnp.concatenate([vv[:, over], ones], axis=1)
                acc = jnp.dot(p, both, preferred_element_type=jnp.float32)
                obuf[part, over] = (acc[:, :VDIM] / acc[:, VDIM:]).astype(jnp.bfloat16)
        done = pl.ds(pl.multiple_of(j * 2 * VDIM, 128), 2 * VDIM)
        pltpu.make_async_copy(obuf.at[:, done], out_h.at[:, done], osem.at[j]).start()

    for dz in range(1, Z):
        z_copy(dz).wait_send()
    for dz in range(Z):
        for dx in range(1, X):
            x_copy(dz, dx).wait_send()

    for j in range(waited, pieces):
        for d in range(1, Y):
            y_copy(j, d).wait_send()

    @pl.loop(0, pieces)
    def _(j):
        c_copy(j).wait_send()
        for d in range(1, Y):
            f_copy(j, d).wait_send()
        done = pl.ds(pl.multiple_of(j * 2 * VDIM, 128), 2 * VDIM)
        pltpu.make_async_copy(obuf.at[:, done], out_h.at[:, done], osem.at[j]).wait()


def per_device(Y, Z, X, query_latent, q_weight, key_absorb, value_up, branch_latent, lengths, row_depth):
    rows, rank = query_latent.shape
    cols = q_weight.shape[1]
    heads = key_absorb.shape[0]
    share = branch_latent.shape[1]
    length = share * Z * X
    pieces = cols // PAIR
    width = heads * VDIM
    bf = jnp.bfloat16
    dma = pltpu.SemaphoreType.DMA
    anywhere = pl.BlockSpec(memory_space=pl.ANY)
    return pl.pallas_call(
        functools.partial(kernel, Y, Z, X),
        out_shape=jax.ShapeDtypeStruct((rows, width), bf),
        in_specs=[anywhere] * 5 + [pl.BlockSpec(memory_space=pltpu.VMEM), pl.BlockSpec(memory_space=pltpu.SMEM)],
        out_specs=anywhere,
        scratch_shapes=[
            pltpu.VMEM((rank, cols), bf),
            pltpu.VMEM((rows, rank), bf),
            pltpu.VMEM((heads * NOPE, KVR), bf),
            pltpu.VMEM((KVR, width), bf),
            pltpu.VMEM((length, KVR + ROPE), bf),
            pltpu.VMEM((heads, WIDE, length), bf),
            pltpu.VMEM((length, width), bf),
            pltpu.VMEM((rows, width), bf),
            pltpu.VMEM((rows, PAIR), bf),
            pltpu.VMEM((rows, 1), jnp.int32),
            dma((Y - 1, pieces)), dma((Y - 1, pieces)),
            dma((pieces,)), dma((pieces,)),
            dma((Y - 1, pieces)), dma((Y - 1, pieces)),
            dma((Z - 1,)), dma((Z - 1,)),
            dma((Z, X - 1)), dma((Z, X - 1)),
            dma((4,)), dma((heads,)), dma((pieces,)),
        ],
        compiler_params=pltpu.CompilerParams(
            collective_id=0, has_side_effects=True, vmem_limit_bytes=60 * 1024 * 1024),
    )(query_latent, q_weight, key_absorb.reshape(heads * NOPE, KVR), value_up,
      branch_latent.reshape(share, KVR + ROPE), row_depth.reshape(1, rows), lengths)


def solution(mesh):
    placed = (
        P("grp", None),
        P("grp", "head"),
        P("head", None, None),
        P("head", None, None),
        P("grp", "head", None),
        P("grp"),
        P("grp"),
    )
    across = math.isqrt(mesh.shape["head"] // 2)
    return jax.shard_map(
        functools.partial(per_device, mesh.shape["grp"] // 2, mesh.shape["head"] // across, across),
        mesh=mesh, in_specs=placed, out_specs=P("grp", "head"), check_vma=False
    )
```

time: 342 us -> 87.6 us (0.26)
  the two profiles are of different devices: /device:TPU:0 before, /device:TPU:24 now
where the time goes in v1:
time: 87.6 us; the launch traced here: 87.5 us
  Pallas kernels  83.6 us (95%)
  local copies, waits for them, and re-layouts  3.16 us (4%)
    pallas_call x1, Pallas kernels, per_device(): pl.pallas_call(functools.partial(kernel, Y, Z, X), out_shape=jax.ShapeDty...  83.6 us
    unnamed x1, local copies, waits for them, and re-layouts  3.16 us

profile of v1, /device:TPU:24, one launch (start us, length us, event | category | flops | bytes accessed | tf_op | source)
XLA Modules:
  0.0 87.5 jit_solution(17142608201093465534)
XLA Ops:
  0.7 83.6 %shard_map.73 = bf16[512,2048]{1,0:T(8,128)(2,1)} custom-call(bf16[512,1536]{1,0:T(8,128)(2,1)} %ql_h.1, bf16[384,3072]{1,0:T(8,128)(2,1)} %w_h.1, bf16[2048,512]{1,0:T(8,128)(2,1)} %bitcast.3, bf16[16,512,128]{2,1,0:T(8,128)(2,1)} %vu_h.1, bf16[192,576]{1,0:T(8,128)(2,1)} %bitcast.4, s32[1,512]{1,0:T(1,128)} %bitcast.5, s32[1]{0:T(128)S(6)} %copy.9.lens), custom_call_target="tpu_custom_call" | custom-call | tf_op jit(solution)/shard_map/pallas_call | solution.py:253
  84.3 3.2 %copy.10 = bf16[512,2048]{1,0:T(8,128)(2,1)} copy(bf16[512,2048]{1,0:T(8,128)(2,1)} %shard_map.73) | data formatting | bytes 4194304

commit v2 on v1

--- a/solution.py
+++ b/solution.py
@@ -22,12 +22,12 @@
 
 
 def kernel(Y, Z, X, ql_h, w_h, ka_h, vu_h, lat_h, dep, lens, out_h,
-           wbuf, ql, ka, vu, lat, kt, vv, obuf, qb, seen,
+           wbuf, ql, ka, vu, vut, lat, kx, vt, obuf, qb, bias,
            ysend, yrecv, csend, crecv, fsend, frecv,
            zsend, zrecv, xsend, xrecv, lsem, vsem, osem):
     rows, rank = ql.shape
     depth, cols = w_h.shape
-    heads = vu_h.shape[0]
+    heads = vu.shape[0]
     share = lat_h.shape[0]
     length = lat.shape[0]
     pieces = cols // PAIR
@@ -92,12 +92,16 @@
 
     local = [
         pltpu.make_async_copy(lat_h, shard(h), lsem.at[0]),
-        pltpu.make_async_copy(ka_h, ka, lsem.at[1]),
+        pltpu.make_async_copy(vu_h, vu, lsem.at[1]),
         pltpu.make_async_copy(ql_h, ql, lsem.at[2]),
         pltpu.make_async_copy(w_h, wbuf.at[pl.ds(pl.multiple_of(g * depth, 16), depth)], lsem.at[3]),
     ]
     for i in range(heads):
-        local.append(pltpu.make_async_copy(vu_h.at[i], vu.at[:, pl.ds(i * VDIM, VDIM)], vsem.at[i]))
+        for e in range(2):
+            src = (e + i) % 2
+            local.append(pltpu.make_async_copy(
+                ka_h.at[pl.ds(i * NOPE + src * ROPE, ROPE)],
+                ka.at[pl.ds(i * NOPE + e * ROPE, ROPE)], vsem.at[2 * i + e]))
     for copy in local:
         copy.start()
     pl.semaphore_wait(barrier, len(peers))
@@ -115,42 +119,52 @@
     for j in range(1, min(AHEAD, pieces)):
         start_piece(j)
 
-    row = lax.broadcasted_iota(jnp.int32, (rows, rows), 0)
-    col = lax.broadcasted_iota(jnp.int32, (rows, rows), 1)
-    kept = jnp.minimum(dep[...], lens[0]).astype(jnp.float32)
-    seen[...] = jnp.sum(jnp.where(row == col, kept, 0.0), axis=1, keepdims=True).astype(jnp.int32)
+    kept = jnp.minimum(dep[...], lens[0])
+    step = 128
+
+    @pl.loop(0, length // step)
+    def _(i):
+        at = pl.ds(pl.multiple_of(i * step, step), step)
+        place = lax.broadcasted_iota(jnp.int32, (step, rows), 0) + i * step
+        bias[at, :] = jnp.where(place < kept, 0.0, jnp.float32(-1e30))
 
     for copy in local:
         copy.wait()
 
-    eye = (lax.broadcasted_iota(jnp.int32, (ROPE, ROPE), 0)
-           == lax.broadcasted_iota(jnp.int32, (ROPE, ROPE), 1)).astype(jnp.bfloat16)
+    @pl.loop(0, heads)
+    def _(i):
+        vut[pl.ds(pl.multiple_of(i * VDIM, 16), VDIM), :] = vu[i].T
+
+    source = lax.broadcasted_iota(jnp.int32, (ROPE, WIDE), 0)
+    target = lax.broadcasted_iota(jnp.int32, (ROPE, WIDE), 1)
+    spread = ((source == target) | (source + WIDE - ROPE == target)).astype(jnp.bfloat16)
     at_once = 4
 
     def keys_values(index):
         at = pl.ds(pl.multiple_of(index * chunk, 128), chunk)
-        rope = lax.dot_general(eye, lat[at, KVR:], NT, preferred_element_type=jnp.float32).astype(jnp.bfloat16)
-        blank = jnp.zeros((ROPE, chunk), jnp.bfloat16)
+        rope = jnp.dot(lat[at, KVR:], spread, preferred_element_type=jnp.float32)
+        first = rope[:, :NOPE].astype(jnp.bfloat16)
+        low = lax.broadcasted_iota(jnp.int32, (chunk, NOPE), 1) < ROPE
 
         @pl.loop(0, heads // at_once)
         def _(i):
             latent = lat[at, :KVR]
             wide = at_once * NOPE
-            keys = lax.dot_general(ka[pl.ds(pl.multiple_of(i * wide, 16), wide), :], latent, NT,
-                                   preferred_element_type=jnp.float32).astype(jnp.bfloat16)
+            over = pl.ds(pl.multiple_of(i * wide, 128), wide)
+            keys = lax.dot_general(latent, ka[over, :], NT, preferred_element_type=jnp.float32)
             for e in range(at_once):
-                own = keys[e * NOPE:(e + 1) * NOPE]
-                head = i * at_once + e
+                own = keys[:, e * NOPE:(e + 1) * NOPE]
+                base = (i * at_once + e) * WIDE
+                left = pl.ds(pl.multiple_of(base, 128), NOPE)
+                right = pl.ds(pl.multiple_of(base + NOPE, 128), NOPE)
                 if e % 2 == 0:
-                    kt[head, 0:NOPE, at] = own
-                    kt[head, NOPE:HEAD, at] = rope
-                    kt[head, HEAD:WIDE, at] = blank
+                    kx[at, left] = own.astype(jnp.bfloat16)
+                    kx[at, right] = first
                 else:
-                    kt[head, 0:ROPE, at] = blank
-                    kt[head, ROPE:HEAD, at] = own
-                    kt[head, HEAD:WIDE, at] = rope
-            over = pl.ds(pl.multiple_of(i * wide, 128), wide)
-            vv[at, over] = jnp.dot(latent, vu[:, over], preferred_element_type=jnp.float32).astype(jnp.bfloat16)
+                    kx[at, left] = jnp.where(low, 0.0, own).astype(jnp.bfloat16)
+                    kx[at, right] = jnp.where(low, own, rope[:, NOPE:]).astype(jnp.bfloat16)
+            vt[over, at] = lax.dot_general(vut[over, :], latent, NT,
+                                           preferred_element_type=jnp.float32).astype(jnp.bfloat16)
 
     def take_x(dz):
         for dx in range(1, X):
@@ -161,8 +175,24 @@
         for dx in range(1, X):
             x_copy(dz, dx).start()
 
+    half = rows // 2
+
+    def hand_on(j):
+        for d in range(1, Y):
+            y_copy(j, d).wait_recv()
+            f_copy(j, d).start()
+
+    def project(j):
+        c_copy(j).wait_recv()
+        for d in range(1, Y):
+            f_copy(j, d).wait_recv()
+        weight = pl.ds(pl.multiple_of(j * PAIR, 128), PAIR)
+        q = jnp.dot(ql[...], wbuf[:, weight], preferred_element_type=jnp.float32)
+        qb[:, weight] = (q * jnp.float32(SCALE)).astype(jnp.bfloat16)
+
     waited = 0
     started = min(AHEAD, pieces)
+    early = min(chunks - 1, pieces - 1)
     if not whole_rows:
         for dz in range(1, Z):
             pass_on(dz)
@@ -173,9 +203,11 @@
             if k + 1 < Z:
                 pass_on(k + 1)
             take_x(k)
-            keys_values(lax.rem(z + Z - k, Z))
-        else:
-            keys_values(k)
+        if 1 <= k <= early:
+            hand_on(k - 1)
+        keys_values(lax.rem(z + Z - k, Z) if whole_rows else k)
+        if 1 <= k <= early:
+            project(k - 1)
         if started < pieces:
             for d in range(1, Y):
                 y_copy(waited, d).wait_send()
@@ -186,37 +218,42 @@
         start_piece(started)
         started += 1
 
-    half = rows // 2
-    ones = jnp.ones((length, VDIM), jnp.bfloat16)
+    ones = jnp.ones((16, length), jnp.bfloat16)
 
     @pl.loop(0, pieces)
     def _(j):
-        for d in range(1, Y):
-            y_copy(j, d).wait_recv()
-            f_copy(j, d).start()
-        c_copy(j).wait_recv()
-        for d in range(1, Y):
-            f_copy(j, d).wait_recv()
-        weight = pl.ds(pl.multiple_of(j * PAIR, 128), PAIR)
-        for r in range(2):
+        @pl.when((j + 1 >= early) & (j + 1 < pieces - 1))
+        def _():
+            hand_on(j + 1)
+
+        @pl.when(j == pieces - 1)
+        def _():
+            hand_on(j)
+
+        @pl.when(j >= early)
+        def _():
+            project(j)
+
+        blocks = [(r, e) for r in range(2) for e in range(2)]
+
+        def scores(r, e):
+            query = qb[r * half:(r + 1) * half, pl.ds(pl.multiple_of(j * PAIR + e * NOPE, 128), WIDE)]
+            key = kx[:, pl.ds(pl.multiple_of((j * 2 + e) * WIDE, 128), WIDE)]
+            return lax.dot_general(key, query, NT, preferred_element_type=jnp.float32)
+
+        ahead = scores(*blocks[0])
+        for i, (r, e) in enumerate(blocks):
+            s = ahead
+            if i + 1 < len(blocks):
+                ahead = scores(*blocks[i + 1])
             part = slice(r * half, (r + 1) * half)
-            q = jnp.dot(ql[part, :], wbuf[:, weight], preferred_element_type=jnp.float32)
-            qb[part, :] = (q * jnp.float32(SCALE)).astype(jnp.bfloat16)
-        for r in range(2):
-            part = slice(r * half, (r + 1) * half)
-            limit = seen[part, :]
-            for e in range(2):
-                head = j * 2 + e
-                q = qb[part, 0:WIDE] if e == 0 else qb[part, NOPE:PAIR]
-                s = jnp.dot(q, kt[head], preferred_element_type=jnp.float32)
-                place = lax.broadcasted_iota(jnp.int32, s.shape, 1)
-                s = jnp.where(place < limit, s, jnp.float32(-1e30))
-                peak = jnp.max(s, axis=1, keepdims=True)
-                p = jnp.exp2(s - peak).astype(jnp.bfloat16)
-                over = pl.ds(pl.multiple_of(head * VDIM, 128), VDIM)
-                both = jnp.concatenate([vv[:, over], ones], axis=1)
-                acc = jnp.dot(p, both, preferred_element_type=jnp.float32)
-                obuf[part, over] = (acc[:, :VDIM] / acc[:, VDIM:]).astype(jnp.bfloat16)
+            s = s + bias[:, part]
+            peak = jnp.max(s, axis=0, keepdims=True)
+            p = jnp.exp2(s - peak).astype(jnp.bfloat16)
+            over = pl.ds(pl.multiple_of((j * 2 + e) * VDIM, 128), VDIM)
+            both = jnp.concatenate([vt[over, :], ones], axis=0)
+            acc = jnp.dot(both, p, preferred_element_type=jnp.float32)
+            obuf[part, over] = (acc[:VDIM] / acc[VDIM:VDIM + 1]).T.astype(jnp.bfloat16)
         done = pl.ds(pl.multiple_of(j * 2 * VDIM, 128), 2 * VDIM)
         pltpu.make_async_copy(obuf.at[:, done], out_h.at[:, done], osem.at[j]).start()
 
@@ -259,19 +296,20 @@
             pltpu.VMEM((rank, cols), bf),
             pltpu.VMEM((rows, rank), bf),
             pltpu.VMEM((heads * NOPE, KVR), bf),
-            pltpu.VMEM((KVR, width), bf),
+            pltpu.VMEM((heads, KVR, VDIM), bf),
+            pltpu.VMEM((width, KVR), bf),
             pltpu.VMEM((length, KVR + ROPE), bf),
-            pltpu.VMEM((heads, WIDE, length), bf),
-            pltpu.VMEM((length, width), bf),
+            pltpu.VMEM((length, heads * WIDE), bf),
+            pltpu.VMEM((width, length), bf),
             pltpu.VMEM((rows, width), bf),
-            pltpu.VMEM((rows, PAIR), bf),
-            pltpu.VMEM((rows, 1), jnp.int32),
+            pltpu.VMEM((rows, cols), bf),
+            pltpu.VMEM((length, rows), jnp.float32),
             dma((Y - 1, pieces)), dma((Y - 1, pieces)),
             dma((pieces,)), dma((pieces,)),
             dma((Y - 1, pieces)), dma((Y - 1, pieces)),
             dma((Z - 1,)), dma((Z - 1,)),
             dma((Z, X - 1)), dma((Z, X - 1)),
-            dma((4,)), dma((heads,)), dma((pieces,)),
+            dma((4,)), dma((2 * heads,)), dma((pieces,)),
         ],
         compiler_params=pltpu.CompilerParams(
             collective_id=0, has_side_effects=True, vmem_limit_bytes=60 * 1024 * 1024),

time: 87.6 us -> 85 us (0.970)
  the two profiles are of different devices: /device:TPU:24 before, /device:TPU:25 now
where the time goes in v2:
time: 85 us; the launch traced here: 84.8 us
  Pallas kernels  81 us (95%)
  local copies, waits for them, and re-layouts  3.16 us (4%)
    pallas_call x1, Pallas kernels, per_device(): pl.pallas_call(functools.partial(kernel, Y, Z, X), out_shape=jax.ShapeDty...  81 us
    unnamed x1, local copies, waits for them, and re-layouts  3.16 us

profile of v2, /device:TPU:25, one launch (start us, length us, event | category | flops | bytes accessed | tf_op | source)
XLA Modules:
  0.0 84.8 jit_solution(5150207226397671053)
XLA Ops:
  0.7 81.0 %shard_map.73 = bf16[512,2048]{1,0:T(8,128)(2,1)} custom-call(bf16[512,1536]{1,0:T(8,128)(2,1)} %ql_h.1, bf16[384,3072]{1,0:T(8,128)(2,1)} %w_h.1, bf16[2048,512]{1,0:T(8,128)(2,1)} %bitcast.3, bf16[16,512,128]{2,1,0:T(8,128)(2,1)} %vu_h.1, bf16[192,576]{1,0:T(8,128)(2,1)} %bitcast.4, s32[1,512]{1,0:T(1,128)} %bitcast.5, s32[1]{0:T(128)S(6)} %copy.9.lens), custom_call_target="tpu_custom_call" | custom-call | tf_op jit(solution)/shard_map/pallas_call | solution.py:290
  81.7 3.2 %copy.10 = bf16[512,2048]{1,0:T(8,128)(2,1)} copy(bf16[512,2048]{1,0:T(8,128)(2,1)} %shard_map.73) | data formatting | bytes 4194304

commit v3 on v2

--- a/solution.py
+++ b/solution.py
@@ -15,7 +15,7 @@
 HEAD = NOPE + ROPE
 PAIR = 2 * HEAD
 WIDE = 256
-AHEAD = 3
+AHEAD = 4
 MESH = pl.DeviceIdType.MESH
 NT = (((1,), (1,)), ((), ()))
 SCALE = (HEAD ** -0.5) * math.log2(math.e)
@@ -24,7 +24,7 @@
 def kernel(Y, Z, X, ql_h, w_h, ka_h, vu_h, lat_h, dep, lens, out_h,
            wbuf, ql, ka, vu, vut, lat, kx, vt, obuf, qb, bias,
            ysend, yrecv, csend, crecv, fsend, frecv,
-           zsend, zrecv, xsend, xrecv, lsem, vsem, osem):
+           upsend, uprecv, downsend, downrecv, xsend, xrecv, lsem, vsem, osem):
     rows, rank = ql.shape
     depth, cols = w_h.shape
     heads = vu.shape[0]
@@ -74,15 +74,23 @@
         part = w_part(lax.rem(y + Y - d, Y) * 2 + c, j)
         return remote(part, part, fsend.at[d - 1, j], frecv.at[d - 1, j], other)
 
-    def z_copy(d):
-        return remote(lat_h, shard(h), zsend.at[d - 1], zrecv.at[d - 1], z_at(d))
-
-    def x_copy(dz, dx):
-        if dz == 0:
-            src, dst = lat_h, shard(h)
-        else:
-            src = dst = shard(lax.rem(z + Z - dz, Z) * X + x)
-        return remote(src, dst, xsend.at[dz, dx - 1], xrecv.at[dz, dx - 1], x_at(dx))
+    def up_copy(t):
+        part = shard((z - t + 1) * X + x)
+        return remote(lat_h if t == 1 else part, part, upsend.at[t - 1], uprecv.at[t - 1], z_at(1))
+
+    def down_copy(t):
+        part = shard((z + t - 1) * X + x)
+        return remote(lat_h if t == 1 else part, part, downsend.at[t - 1], downrecv.at[t - 1], z_at(Z - 1))
+
+    def x_copy(layer, dx, own=False):
+        part = shard(layer * X + x)
+        return remote(lat_h if own else part, part, xsend.at[layer, dx - 1], xrecv.at[layer, dx - 1], x_at(dx))
+
+    def sends_up(t):
+        return (z - t + 1 >= 0) & (z + 1 < Z)
+
+    def sends_down(t):
+        return (z + t - 1 < Z) & (z >= 1)
 
     peers = ([y_at(d) for d in range(1, Y)] + [other]
              + [z_at(d) for d in range(1, Z)] + [x_at(d) for d in range(1, X)])
@@ -113,9 +121,20 @@
 
     start_piece(0)
     for dx in range(1, X):
-        x_copy(0, dx).start()
-    for d in range(1, Z):
-        z_copy(d).start()
+        x_copy(z, dx, True).start()
+
+    def pass_up(t):
+        @pl.when(sends_up(t))
+        def _():
+            up_copy(t).start()
+
+    def pass_down(t):
+        @pl.when(sends_down(t))
+        def _():
+            down_copy(t).start()
+
+    pass_up(1)
+    pass_down(1)
     for j in range(1, min(AHEAD, pieces)):
         start_piece(j)
 
@@ -166,14 +185,37 @@
             vt[over, at] = lax.dot_general(vut[over, :], latent, NT,
                                            preferred_element_type=jnp.float32).astype(jnp.bfloat16)
 
-    def take_x(dz):
+    def take_x(layer):
         for dx in range(1, X):
-            x_copy(dz, dx).wait_recv()
-
-    def pass_on(dz):
-        z_copy(dz).wait_recv()
-        for dx in range(1, X):
-            x_copy(dz, dx).start()
+            x_copy(layer, dx).wait_recv()
+
+    def relay(t):
+        @pl.when(z - t >= 0)
+        def _():
+            up_copy(t).wait_recv()
+            if t + 1 < Z:
+                pass_up(t + 1)
+            for dx in range(1, X):
+                x_copy(z - t, dx).start()
+
+        @pl.when(z + t < Z)
+        def _():
+            down_copy(t).wait_recv()
+            if t + 1 < Z:
+                pass_down(t + 1)
+            for dx in range(1, X):
+                x_copy(z + t, dx).start()
+
+    def layers(t):
+        @pl.when(z - t >= 0)
+        def _():
+            take_x(z - t)
+            keys_values(z - t)
+
+        @pl.when(z + t < Z)
+        def _():
+            take_x(z + t)
+            keys_values(z + t)
 
     half = rows // 2
 
@@ -190,33 +232,35 @@
         q = jnp.dot(ql[...], wbuf[:, weight], preferred_element_type=jnp.float32)
         qb[:, weight] = (q * jnp.float32(SCALE)).astype(jnp.bfloat16)
 
-    waited = 0
     started = min(AHEAD, pieces)
-    early = min(chunks - 1, pieces - 1)
-    if not whole_rows:
-        for dz in range(1, Z):
-            pass_on(dz)
-        for dz in range(Z):
-            take_x(dz)
-    for k in range(chunks):
-        if whole_rows:
-            if k + 1 < Z:
-                pass_on(k + 1)
-            take_x(k)
-        if 1 <= k <= early:
-            hand_on(k - 1)
-        keys_values(lax.rem(z + Z - k, Z) if whole_rows else k)
-        if 1 <= k <= early:
-            project(k - 1)
-        if started < pieces:
-            for d in range(1, Y):
-                y_copy(waited, d).wait_send()
-            waited += 1
-            start_piece(started)
-            started += 1
+    early = min(2, pieces - 1)
+    take_x(z)
+    if whole_rows:
+        relay(1)
+        keys_values(z)
+        for t in range(1, Z):
+            if t + 1 < Z:
+                relay(t + 1)
+            if started < pieces:
+                start_piece(started)
+                started += 1
+            layers(t)
+    else:
+        for t in range(1, Z):
+            relay(t)
+        for layer in range(Z):
+            @pl.when(z != layer)
+            def _():
+                take_x(layer)
+        for k in range(chunks):
+            keys_values(k)
     while started < pieces:
         start_piece(started)
         started += 1
+    for j in range(early):
+        hand_on(j)
+    for j in range(early):
+        project(j)
 
     ones = jnp.ones((16, length), jnp.bfloat16)
 
@@ -257,20 +301,23 @@
         done = pl.ds(pl.multiple_of(j * 2 * VDIM, 128), 2 * VDIM)
         pltpu.make_async_copy(obuf.at[:, done], out_h.at[:, done], osem.at[j]).start()
 
-    for dz in range(1, Z):
-        z_copy(dz).wait_send()
-    for dz in range(Z):
+    for t in range(1, Z):
+        @pl.when(sends_up(t))
+        def _():
+            up_copy(t).wait_send()
+
+        @pl.when(sends_down(t))
+        def _():
+            down_copy(t).wait_send()
+    for layer in range(Z):
         for dx in range(1, X):
-            x_copy(dz, dx).wait_send()
-
-    for j in range(waited, pieces):
-        for d in range(1, Y):
-            y_copy(j, d).wait_send()
+            x_copy(layer, dx).wait_send()
 
     @pl.loop(0, pieces)
     def _(j):
         c_copy(j).wait_send()
         for d in range(1, Y):
+            y_copy(j, d).wait_send()
             f_copy(j, d).wait_send()
         done = pl.ds(pl.multiple_of(j * 2 * VDIM, 128), 2 * VDIM)
         pltpu.make_async_copy(obuf.at[:, done], out_h.at[:, done], osem.at[j]).wait()
@@ -307,7 +354,7 @@
             dma((Y - 1, pieces)), dma((Y - 1, pieces)),
             dma((pieces,)), dma((pieces,)),
             dma((Y - 1, pieces)), dma((Y - 1, pieces)),
-            dma((Z - 1,)), dma((Z - 1,)),
+            dma((Z - 1,)), dma((Z - 1,)), dma((Z - 1,)), dma((Z - 1,)),
             dma((Z, X - 1)), dma((Z, X - 1)),
             dma((4,)), dma((2 * heads,)), dma((pieces,)),
         ],

time: 85 us -> 81.1 us (0.954)
  the two profiles are of different devices: /device:TPU:25 before, /device:TPU:0 now
where the time goes in v3:
time: 81.1 us; the launch traced here: 80.9 us
  Pallas kernels  77.1 us (95%)
  local copies, waits for them, and re-layouts  3.16 us (4%)
    pallas_call x1, Pallas kernels, per_device(): pl.pallas_call(functools.partial(kernel, Y, Z, X), out_shape=jax.ShapeDty...  77.1 us
    unnamed x1, local copies, waits for them, and re-layouts  3.16 us

profile of v3, /device:TPU:0, one launch (start us, length us, event | category | flops | bytes accessed | tf_op | source)
XLA Modules:
  0.0 80.9 jit_solution(9656130457668502305)
XLA Ops:
  0.7 77.1 %shard_map.73 = bf16[512,2048]{1,0:T(8,128)(2,1)} custom-call(bf16[512,1536]{1,0:T(8,128)(2,1)} %ql_h.1, bf16[384,3072]{1,0:T(8,128)(2,1)} %w_h.1, bf16[2048,512]{1,0:T(8,128)(2,1)} %bitcast.3, bf16[16,512,128]{2,1,0:T(8,128)(2,1)} %vu_h.1, bf16[192,576]{1,0:T(8,128)(2,1)} %bitcast.4, s32[1,512]{1,0:T(1,128)} %bitcast.5, s32[1]{0:T(128)S(6)} %copy.9.lens), custom_call_target="tpu_custom_call" | custom-call | tf_op jit(solution)/shard_map/pallas_call | solution.py:337
  77.8 3.2 %copy.10 = bf16[512,2048]{1,0:T(8,128)(2,1)} copy(bf16[512,2048]{1,0:T(8,128)(2,1)} %shard_map.73) | data formatting | bytes 4194304

commit v4 on v3

--- a/solution.py
+++ b/solution.py
@@ -15,7 +15,8 @@
 HEAD = NOPE + ROPE
 PAIR = 2 * HEAD
 WIDE = 256
-AHEAD = 4
+AHEAD = 2
+LAG = 2
 MESH = pl.DeviceIdType.MESH
 NT = (((1,), (1,)), ((), ()))
 SCALE = (HEAD ** -0.5) * math.log2(math.e)
@@ -233,6 +234,18 @@
         qb[:, weight] = (q * jnp.float32(SCALE)).astype(jnp.bfloat16)
 
     started = min(AHEAD, pieces)
+    left = set(range(pieces))
+
+    def next_piece(after):
+        nonlocal started
+        if started < pieces:
+            if after >= 0:
+                for d in range(1, Y):
+                    y_copy(after, d).wait_send()
+                left.discard(after)
+            start_piece(started)
+            started += 1
+
     early = min(2, pieces - 1)
     take_x(z)
     if whole_rows:
@@ -241,9 +254,8 @@
         for t in range(1, Z):
             if t + 1 < Z:
                 relay(t + 1)
-            if started < pieces:
-                start_piece(started)
-                started += 1
+            if t % 2 == 1:
+                next_piece(started - 3)
             layers(t)
     else:
         for t in range(1, Z):
@@ -254,9 +266,7 @@
                 take_x(layer)
         for k in range(chunks):
             keys_values(k)
-    while started < pieces:
-        start_piece(started)
-        started += 1
+    next_piece(started - 3)
     for j in range(early):
         hand_on(j)
     for j in range(early):
@@ -266,14 +276,6 @@
 
     @pl.loop(0, pieces)
     def _(j):
-        @pl.when((j + 1 >= early) & (j + 1 < pieces - 1))
-        def _():
-            hand_on(j + 1)
-
-        @pl.when(j == pieces - 1)
-        def _():
-            hand_on(j)
-
         @pl.when(j >= early)
         def _():
             project(j)
@@ -301,6 +303,16 @@
         done = pl.ds(pl.multiple_of(j * 2 * VDIM, 128), 2 * VDIM)
         pltpu.make_async_copy(obuf.at[:, done], out_h.at[:, done], osem.at[j]).start()
 
+        @pl.when((j + 1 >= early) & (j + 1 < pieces))
+        def _():
+            hand_on(j + 1)
+
+        @pl.when(j + started < pieces)
+        def _():
+            for d in range(1, Y):
+                y_copy(j + started - LAG, d).wait_send()
+            start_piece(j + started)
+
     for t in range(1, Z):
         @pl.when(sends_up(t))
         def _():
@@ -313,11 +325,15 @@
         for dx in range(1, X):
             x_copy(layer, dx).wait_send()
 
+    left -= set(range(started - LAG, pieces - LAG))
+    for j in sorted(left):
+        for d in range(1, Y):
+            y_copy(j, d).wait_send()
+
     @pl.loop(0, pieces)
     def _(j):
         c_copy(j).wait_send()
         for d in range(1, Y):
-            y_copy(j, d).wait_send()
             f_copy(j, d).wait_send()
         done = pl.ds(pl.multiple_of(j * 2 * VDIM, 128), 2 * VDIM)
         pltpu.make_async_copy(obuf.at[:, done], out_h.at[:, done], osem.at[j]).wait()

time: 81.1 us -> 87.9 us (1.084); the launches traced: 80.9 us -> 86.6 us
  Pallas kernels: 77.1 us -> 82.8 us
    pallas_call x1, Pallas kernels: 77.1 us -> 82.8 us  [per_device(): pl.pallas_call(functools.partial(kernel, Y, Z, X), out_shape=jax.ShapeDty...]
where the time goes in v4:
time: 87.9 us; the launch traced here: 86.6 us
  Pallas kernels  82.8 us (94%)
  local copies, waits for them, and re-layouts  3.16 us (4%)
    pallas_call x1, Pallas kernels, per_device(): pl.pallas_call(functools.partial(kernel, Y, Z, X), out_shape=jax.ShapeDty...  82.8 us
    unnamed x1, local copies, waits for them, and re-layouts  3.16 us

profile of v4, /device:TPU:0, one launch (start us, length us, event | category | flops | bytes accessed | tf_op | source)
XLA Modules:
  0.0 86.6 jit_solution(11537043934084184559)
XLA Ops:
  0.7 82.8 %shard_map.73 = bf16[512,2048]{1,0:T(8,128)(2,1)} custom-call(bf16[512,1536]{1,0:T(8,128)(2,1)} %ql_h.1, bf16[384,3072]{1,0:T(8,128)(2,1)} %w_h.1, bf16[2048,512]{1,0:T(8,128)(2,1)} %bitcast.3, bf16[16,512,128]{2,1,0:T(8,128)(2,1)} %vu_h.1, bf16[192,576]{1,0:T(8,128)(2,1)} %bitcast.4, s32[1,512]{1,0:T(1,128)} %bitcast.5, s32[1]{0:T(128)S(6)} %copy.9.lens), custom_call_target="tpu_custom_call" | custom-call | tf_op jit(solution)/shard_map/pallas_call | solution.py:353
  83.5 3.2 %copy.10 = bf16[512,2048]{1,0:T(8,128)(2,1)} copy(bf16[512,2048]{1,0:T(8,128)(2,1)} %shard_map.73) | data formatting | bytes 4194304
